TPU v7x, 256 devices: a whole 4x4x8 slice. The times are simulated.
256 devices in a mesh: row: 8 (over x, core), col: 32 (over z, y).
Axes of the slice: x: 4, y: 4, z: 8, core: 2. Of those that a mesh axis runs over, the one named last changes fastest.
Arguments:
- centres: float32 [524288, 64], P(('row', 'col')), may hold values from -6 to 6
- weights: float32 [524288, 64], P(('row', 'col')), may hold values from -0.078125 to 0.078125
- targets: float32 [512, 64], replicated, may hold values from -6 to 6
- batch_index: int32 [512], replicated, may hold values from 0 to 524287
- nystrom_index: int32 [4096], replicated, may hold values from 0 to 524287
- eigvecs: float32 [4096, 1024], P('row', 'col'), may hold values from -0.09375 to 0.09375
- mode_scale: float32 [1024], P('col'), may hold values from 0.02 to 0.2
Outputs:
- residual: float32 [512, 64], replicated
- step: float32 [524288, 64], P(('row', 'col'))
All inputs are finite; a program needn't handle non-finite values.
Results may differ from a plain program's by a relative error of at most 0.0001.
Values sent between devices are 32-bit elements; how exact they have to be, the bound alone decides.
No kernel may reach another device: no remote copies, remote signals or barrier semaphores. Data moves between devices by JAX's collectives and lax.ppermute only.
A program may use at most 128 MiB of HBM per device.

v0:
```python
import jax
import jax.numpy as jnp
from jax import lax
from jax.sharding import PartitionSpec as P

learning_rate = 0.25


def kernel(left, right):
    left_sq = jnp.sum(left * left, axis=1)
    right_sq = jnp.sum(right * right, axis=1)
    inner_prod = jnp.dot(
        left, right.T, precision=lax.Precision.HIGHEST, preferred_element_type=jnp.float32
    )
    return jnp.exp(
        -(left_sq[:, None] + right_sq[None, :] - 2.0 * inner_prod) / float(left.shape[1])
    )


def product(left, right):
    return jnp.dot(left, right, precision=lax.Precision.HIGHEST, preferred_element_type=jnp.float32)


def local(centres, weights, targets, batch_index, nystrom_index, eigvecs, mode_scale):
    rows_dev = centres.shape[0]
    block_rows = eigvecs.shape[0]
    offset = lax.axis_index(("row", "col")) * rows_dev

    def select_rows(index):
        local_rows = index - offset
        inside = (local_rows >= 0) & (local_rows < rows_dev)
        fetched = jnp.take(centres, jnp.clip(local_rows, 0, rows_dev - 1), axis=0)
        return jnp.where(inside[:, None], fetched, 0.0)

    batch_feats, nystrom = lax.psum(
        (select_rows(batch_index), select_rows(nystrom_index)), ("row", "col")
    )
    nys_block = lax.dynamic_slice_in_dim(nystrom, lax.axis_index("row") * block_rows, block_rows, 0)
    kern_batch = kernel(centres, batch_feats)
    partial_pred = lax.dot_general(
        kern_batch,
        weights,
        (((0,), (0,)), ((), ())),
        precision=lax.Precision.HIGHEST,
        preferred_element_type=jnp.float32,
    )
    prediction = lax.psum(partial_pred, ("row", "col"))
    residual = prediction - targets
    gradient = product(kernel(nys_block, batch_feats), residual)
    mode_terms = lax.dot_general(
        eigvecs,
        gradient,
        (((0,), (0,)), ((), ())),
        precision=lax.Precision.HIGHEST,
        preferred_element_type=jnp.float32,
    )
    coeff = mode_scale[:, None] * lax.psum(mode_terms, "row")
    correction = lax.psum(product(eigvecs, coeff), "col")
    direct = product(kern_batch, residual)
    folded = direct - product(
        kernel(centres, nystrom), lax.all_gather(correction, "row", axis=0, tiled=True)
    )
    step = learning_rate * folded
    return (residual, step)


def solution(mesh):
    in_specs = (
        P(("row", "col"), None),
        P(("row", "col"), None),
        P(),
        P(),
        P(),
        P("row", "col"),
        P("col"),
    )
    out_specs = (P(), P(("row", "col"), None))
    return jax.shard_map(local, mesh=mesh, in_specs=in_specs, out_specs=out_specs, check_vma=False)
```

profile of v0, /device:TPU:1, one launch (start us, length us, event | category | flops | bytes accessed | tf_op | source)
XLA Modules:
  0.0 794.1 jit_solution(17117816910413058456)
XLA Ops:
  7.2 0.0 all-reduce.5.cloned.1.call-start
  7.2 0.7 compare_and_fusion.2
  8.0 1.4 copy.9
  9.4 1.0 gather_fusion
  10.4 0.9 select_select_fusion.1
  11.3 0.0 all-reduce.5.cloned.1.call-update
  11.3 0.0 all-reduce.9.cloned.1.call-start
  11.5 14.2 %gather_fusion.1 = f32[4096,64]{1,0:T(8,128)} fusion(f32[2048,64]{1,0:T(8,128)S(1)} %copy.9, s32[4096]{0:T(1024)S(1)} %fusion.21), kind=kCustom, calls=%fused_computation.1 | custom fusion | bytes 2113536 | tf_op jit(solution)/shard_map/jit(_take)/gather | solution.py:32
  25.6 6.1 select_select_fusion
  31.7 0.1 multiply_reduce_fusion.1
  31.7 234.9 %all-reduce.5.cloned.1.call-done = f32[512,64]{1,0:T(8,128)} async-done(((f32[512,64]{1,0:T(8,128)}), f32[512,64]{1,0:T(8,128)}) %all-reduce.5.cloned.1.call-update) | async-done | bytes 131088 | tf_op jit(solution)/shard_map/psum | solution.py:35
  266.6 1.1 multiply_reduce_fusion.3
  267.7 5.0 fusion.13
  272.7 2.0 copy-done.1
  274.8 4.8 fusion.26
  279.6 0.0 all-reduce.9.cloned.1.call-update
  279.6 0.0 all-reduce.7.cloned.1.call-start
  279.7 260.3 %all-reduce.9.cloned.1.call-done = (f32[512,64]{0,1:T(8,128)}, f32[4096,64]{1,0:T(8,128)}) async-done(((f32[512,64]{0,1:T(8,128)}, f32[4096,64]{1,0:T(8,128)}), (f32[512,64]{0,1:T(8,128)}, f32[4096,64]{1,0:T(8,128)})) %all-reduce.9.cloned.1.call-update) | async-done | bytes 1179664 | tf_op jit(solution)/shard_map/psum | solution.py:47
  540.0 1.1 sub.30
  541.1 1.1 multiply_reduce_fusion.2
  542.3 2.1 fusion.18
  544.4 1.0 fusion.28
  545.3 1.1 convolution_bitcast_fusion.1
  546.5 22.5 %psum.38 = f32[32,64]{1,0:T(8,128)S(1)} all-reduce(f32[32,64]{1,0:T(8,128)S(1)} %convolution_bitcast_fusion.1), channel_id=1, replica_groups=mesh['row'=8,'col'=32] {'row'}, use_global_device_ids=true, to_apply=%region_7.8 | all-reduce | flops 2048 | bytes 16384 | tf_op jit(solution)/shard_map/psum | solution.py:57
  569.0 1.9 convolution_bitcast_fusion
  570.8 0.0 all-reduce.7.cloned.1.call-update
  570.9 0.2 all-gather.2.cloned.1.call-start
  571.1 137.1 %all-reduce.7.cloned.1.call-done = f32[512,64]{0,1:T(8,128)} async-done(((f32[512,64]{0,1:T(8,128)}), f32[512,64]{0,1:T(8,128)}) %all-reduce.7.cloned.1.call-update) | async-done | bytes 131088 | tf_op jit(solution)/shard_map/psum | solution.py:58
  708.2 0.6 multiply_reduce_fusion
  708.8 30.2 %fusion.27 = f32[4096,2048]{0,1:T(8,128)} fusion(f32[4096,64]{1,0:T(8,128)S(1)} %copy-done.2, f32[2048,64]{0,1:T(8,128)S(1)} %copy-done.3), kind=kOutput, calls=%fused_computation.47 | convolution fusion | flops 6442450944 | bytes 35127296 | tf_op jit(solution)/shard_map/dot_general | solution.py:12
  739.1 42.7 %fusion.3 = f32[2048,64]{0,1:T(8,128)S(1)} fusion(f32[4096,64]{0,1:T(8,128)} %all-gather.2.cloned.1.call-done, f32[4096,2048]{0,1:T(8,128)} %fusion.27, f32[4096]{0:T(1024)S(1)} %multiply_reduce_fusion, f32[2048]{0:T(1024)S(1)} %multiply_reduce_fusion.1), kind=kOutput, calls=%fused_computation.6 | convolution fusion | flops 6484393984 | bytes 35151872 | tf_op jit(solution)/shard_map/dot_general | solution.py:21
  781.8 5.8 fusion.14
  (20 shorter events, 0.1 us)
Async XLA Ops:
  7.2 267.6 %copy-start = (f32[2048,64]{0,1:T(8,128)S(1)}, f32[2048,64]{0,1:T(8,128)}, u32[]{:S(2)}) copy-start(f32[2048,64]{0,1:T(8,128)} %param.8) | copy-start | bytes 1572868
  7.2 4.2 copy-start.6
  7.2 259.4 %all-reduce.5.cloned.1.call-start = ((), (), s32[]{:S(2)}) async-start(), calls=%async_computation | async-start | bytes 524288 | tf_op jit(solution)/shard_map/psum | solution.py:35
  11.3 528.6 %all-reduce.9.cloned.1.call-start = ((), (), s32[]{:S(2)}) async-start(), calls=%async_computation.3 | async-start | bytes 4456448 | tf_op jit(solution)/shard_map/psum | solution.py:47
  25.6 6.1 copy-start.3
  272.7 2.0 copy-start.1
  274.8 267.5 %copy-start.5 = (f32[512,64]{1,0:T(8,128)S(1)}, f32[512,64]{1,0:T(8,128)}, u32[]{:S(2)}) copy-start(f32[512,64]{1,0:T(8,128)} %all-reduce.5.cloned.1.call-done) | copy-start | bytes 393220
  279.6 289.3 %copy-start.7 = (f32[32]{0:T(128)S(1)}, f32[32]{0:T(128)}, u32[]{:S(2)}) copy-start(f32[32]{0:T(128)} %param.13) | copy-start | bytes 388
  279.6 428.6 %all-reduce.7.cloned.1.call-start = ((), (), s32[]{:S(2)}) async-start(), calls=%async_computation.1 | async-start | bytes 262144 | tf_op jit(solution)/shard_map/psum | solution.py:58
  540.0 168.3 %copy-start.2 = (f32[4096,64]{1,0:T(8,128)S(1)}, f32[4096,64]{1,0:T(8,128)}, u32[]{:S(2)}) copy-start(f32[4096,64]{1,0:T(8,128)} %get-tuple-element.3) | copy-start | bytes 3145732
  541.1 240.7 %copy-start.4 = (f32[512,64]{0,1:T(8,128)}, f32[512,64]{0,1:T(8,128)S(1)}, u32[]{:S(2)}) copy-start(f32[512,64]{0,1:T(8,128)S(1)} %sub.30) | copy-start | bytes 393220
  570.9 168.2 %all-gather.2.cloned.1.call-start = ((), (), s32[]{:S(2)}) async-start(), calls=%async_computation.2 | async-start | bytes 1179648 | tf_op jit(solution)/shard_map/all_gather | solution.py:61
Sparse Core Ops, SparseCore 0:
  14.1 252.5 all-reduce.4
  279.8 260.1 all-reduce.8
  571.0 137.1 all-reduce.6
  710.0 28.3 all-gather.1
where the time goes:
time: 798 us; the launch traced here: 794 us
  waiting for transfers between devices  632 us (79%)
  matrix products  94.6 us (12%)
  blocking collectives  22.5 us (3%)
  local copies, waits for them, and re-layouts  18.6 us (2%)
  between operations  13.9 us (2%)
  other arithmetic  11.8 us (1%)
    psum x1, waiting for transfers between devices, local(): prediction = lax.psum(partial_pred, ('row', 'col'))  260 us
    psum x1, waiting for transfers between devices, local(): lax.psum((select_rows(batch_index), select_rows(nystrom_index)), ('row',...  235 us
    psum x1, waiting for transfers between devices, local(): correction = lax.psum(product(eigvecs, coeff), 'col')  137 us
    dot_general x4, matrix products, product(): jnp.dot(left, right, precision=lax.Precision.HIGHEST, preferred_element_t...  51.3 us
    dot_general x3, matrix products, kernel(): jnp.dot(left, right.T, precision=lax.Precision.HIGHEST, preferred_element...  37.3 us
    psum x1, blocking collectives, local(): coeff = mode_scale[:, None] * lax.psum(mode_terms, 'row')  22.5 us
  transfers between devices with their start and end apart: 4, of which 3 were waited for; matrix products, arithmetic and copies ran while one was open for 6% of the time, Pallas kernels for 0%

commit v1 on v0

v1 whole, which is shorter than its diff:
```python
import functools

import jax
import jax.numpy as jnp
from jax import lax
from jax.experimental import pallas as pl
from jax.experimental.pallas import tpu as pltpu
from jax.sharding import Mesh
from jax.sharding import PartitionSpec as P

F32 = jnp.float32
BF16 = jnp.bfloat16
ROW = ("x", "core")
COL = ("z", "y")
CHIPS = ("x", "z", "y")
ALL = ("x", "core", "z", "y")
NX, NCORE, NROW, NCOL, NCHIPS = 4, 2, 8, 32, 128
FEATS, OUTS, BATCH, NYS, MODES = 64, 64, 512, 4096, 32
PDEV = 2048
RATE = 0.25
MIB = 1024 * 1024


def params(mib=48, grid=1):
    return pltpu.CompilerParams(
        vmem_limit_bytes=mib * MIB, dimension_semantics=("arbitrary",) * grid
    )


def cost(flops, nbytes, trans=0):
    return pl.CostEstimate(flops=int(flops), bytes_accessed=int(nbytes), transcendentals=int(trans))


def dot(a, b):
    return lax.dot_general(a, b, (((1,), (0,)), ((), ())), preferred_element_type=F32)


def dot_nt(a, b):
    return lax.dot_general(a, b, (((1,), (1,)), ((), ())), preferred_element_type=F32)


def split2(v):
    hi = v.astype(BF16)
    lo = (v - hi.astype(F32)).astype(BF16)
    return hi, lo


def split3(v):
    hi = v.astype(BF16).astype(F32)
    rest = v - hi
    mid = rest.astype(BF16).astype(F32)
    low = (rest - mid).astype(BF16).astype(F32)
    return hi, mid, low


def kern(a, bt):
    ah, am, al = split3(a)
    bh, bm, bl = split3(bt)
    a1 = jnp.concatenate([ah, ah, am], axis=1).astype(BF16)
    a2 = jnp.concatenate([am, ah, al], axis=1).astype(BF16)
    b1 = jnp.concatenate([bh, bm, bh], axis=0).astype(BF16)
    b2 = jnp.concatenate([bm, bl, bh], axis=0).astype(BF16)
    inner = dot(a1, b1) + dot(a2, b2)
    asq = jnp.sum(a * a, axis=1, keepdims=True)
    bsq = jnp.sum(bt * bt, axis=0, keepdims=True)
    return jnp.exp((asq + bsq - 2.0 * inner) * (-1.0 / FEATS))


def select_kernel(index_ref, cent_ref, out_ref, parts):
    @pl.when(pl.program_id(0) == 0)
    def _():
        hi, mid, low = split3(cent_ref[...].T)
        parts[...] = jnp.concatenate([hi, mid, low], axis=0).astype(BF16)

    width = out_ref.shape[1]
    place = lax.broadcasted_iota(jnp.int32, (PDEV, width), 0)
    chosen = jnp.where(place == index_ref[...], 1.0, 0.0).astype(BF16)
    found = dot(parts[...], chosen)
    out_ref[...] = found[:FEATS] + found[FEATS : 2 * FEATS] + found[2 * FEATS :]


def select(index, centres):
    n = index.shape[1]
    block = 512
    return pl.pallas_call(
        select_kernel,
        grid=(n // block,),
        in_specs=[
            pl.BlockSpec((1, block), lambda i: (0, i)),
            pl.BlockSpec((PDEV, FEATS), lambda i: (0, 0)),
        ],
        out_specs=pl.BlockSpec((FEATS, block), lambda i: (0, i)),
        out_shape=jax.ShapeDtypeStruct((FEATS, n), F32),
        scratch_shapes=[pltpu.VMEM((3 * FEATS, PDEV), BF16)],
        compiler_params=params(),
        cost_estimate=cost(2 * 192 * PDEV * n, PDEV * 256 + n * 256),
        name="select",
    )(index, centres)


def add_spread_kernel(in_ref, out_ref):
    total = in_ref[0]
    for i in range(1, in_ref.shape[0]):
        total = total + in_ref[i]
    for i in range(out_ref.shape[0]):
        out_ref[i] = total


def add_spread(parts, copies):
    return pl.pallas_call(
        add_spread_kernel,
        out_shape=jax.ShapeDtypeStruct((copies,) + parts.shape[1:], F32),
        compiler_params=params(grid=0),
        cost_estimate=cost(parts.size, parts.size * 4 + parts.size // parts.shape[0] * copies * 4),
        name="add_spread",
    )(parts)


def add_tiles_kernel(in_ref, out_ref):
    total = in_ref[0]
    for i in range(1, in_ref.shape[0]):
        total = total + in_ref[i]
    for c in range(NCOL):
        out_ref[c] = total[:, c * 128 : (c + 1) * 128]


def add_tiles(parts):
    return pl.pallas_call(
        add_tiles_kernel,
        out_shape=jax.ShapeDtypeStruct((NCOL, 8, 128), F32),
        compiler_params=params(grid=0),
        cost_estimate=cost(parts.size, parts.size * 5),
        name="add_tiles",
    )(parts)


def place_tiles(core_ref, own_ref, other_ref, out_ref):
    mine = core_ref[0]
    for x in range(NX):
        for part, core in ((own_ref, mine), (other_ref, 1 - mine)):
            at = pl.multiple_of((2 * x + core) * 8, 8)
            for c in range(NCOL):
                out_ref[pl.ds(at, 8), c * 128 : (c + 1) * 128] = part[x * NCOL + c]


def assemble(core, own, other):
    return pl.pallas_call(
        place_tiles,
        in_specs=[
            pl.BlockSpec(memory_space=pltpu.SMEM),
            pl.BlockSpec(memory_space=pltpu.VMEM),
            pl.BlockSpec(memory_space=pltpu.VMEM),
        ],
        out_shape=jax.ShapeDtypeStruct((FEATS, NYS), F32),
        compiler_params=params(grid=0),
        cost_estimate=cost(0, 2 * MIB),
        name="assemble",
    )(core, own, other)


def batch_kernel(cent_ref, batch_ref, wts_ref, pred_ref, hi_ref, lo_ref):
    k = kern(cent_ref[...], batch_ref[...])
    khi, klo = split2(k)
    hi_ref[...] = khi
    lo_ref[...] = klo
    whi, wlo = split2(wts_ref[...].T)
    both = dot(jnp.concatenate([whi, wlo], axis=0), khi)
    part = both[:OUTS] + both[OUTS:] + dot(whi, klo)

    @pl.when(pl.program_id(0) == 0)
    def _():
        pred_ref[...] = part

    @pl.when(pl.program_id(0) > 0)
    def _():
        pred_ref[...] += part


def batch_products(centres, batch_t, weights):
    rows = 512
    return pl.pallas_call(
        batch_kernel,
        grid=(PDEV // rows,),
        in_specs=[
            pl.BlockSpec((rows, FEATS), lambda i: (i, 0)),
            pl.BlockSpec((FEATS, BATCH), lambda i: (0, 0)),
            pl.BlockSpec((rows, OUTS), lambda i: (i, 0)),
        ],
        out_specs=[
            pl.BlockSpec((OUTS, BATCH), lambda i: (0, 0)),
            pl.BlockSpec((rows, BATCH), lambda i: (i, 0)),
            pl.BlockSpec((rows, BATCH), lambda i: (i, 0)),
        ],
        out_shape=[
            jax.ShapeDtypeStruct((OUTS, BATCH), F32),
            jax.ShapeDtypeStruct((PDEV, BATCH), BF16),
            jax.ShapeDtypeStruct((PDEV, BATCH), BF16),
        ],
        compiler_params=params(),
        cost_estimate=cost(6e9, 6 * MIB, PDEV * BATCH),
        name="batch_products",
    )(centres, batch_t, weights)


def modes_kernel(batch_ref, nys_ref, eig_ref, scale_ref, out_ref):
    k = kern(batch_ref[...].T, nys_ref[...])
    khi, klo = split2(k)
    ehi, elo = split2(eig_ref[0])
    part = dot_nt(khi, ehi) + dot_nt(khi, elo) + dot_nt(klo, ehi)
    step = pl.program_id(0)

    @pl.when(step == 0)
    def _():
        out_ref[...] = part

    @pl.when(step > 0)
    def _():
        out_ref[...] += part

    @pl.when(step == NROW - 1)
    def _():
        out_ref[...] = out_ref[...] * scale_ref[...]


def mode_products(batch_t, nys_t, eig, scale):
    block = NYS // NROW
    return pl.pallas_call(
        modes_kernel,
        grid=(NROW,),
        in_specs=[
            pl.BlockSpec((FEATS, BATCH), lambda i: (0, 0)),
            pl.BlockSpec((FEATS, block), lambda i: (0, i)),
            pl.BlockSpec((1, MODES, block), lambda i: (i, 0, 0)),
            pl.BlockSpec((1, MODES), lambda i: (0, 0)),
        ],
        out_specs=pl.BlockSpec((BATCH, MODES), lambda i: (0, 0)),
        out_shape=jax.ShapeDtypeStruct((BATCH, MODES), F32),
        compiler_params=params(),
        cost_estimate=cost(1e10, 3 * MIB, NYS * BATCH),
        name="mode_products",
    )(batch_t, nys_t, eig, scale)


def nys_kernel(cent_ref, nys_ref, hi_ref, lo_ref):
    khi, klo = split2(kern(cent_ref[...], nys_ref[...]))
    hi_ref[...] = khi
    lo_ref[...] = klo


def nys_parts(centres, nys_t):
    rows, block = 512, 1024
    shape = jax.ShapeDtypeStruct((PDEV, NYS), BF16)
    return pl.pallas_call(
        nys_kernel,
        grid=(PDEV // rows, NYS // block),
        in_specs=[
            pl.BlockSpec((rows, FEATS), lambda i, j: (i, 0)),
            pl.BlockSpec((FEATS, block), lambda i, j: (0, j)),
        ],
        out_specs=[pl.BlockSpec((rows, block), lambda i, j: (i, j))] * 2,
        out_shape=[shape, shape],
        compiler_params=params(grid=2),
        cost_estimate=cost(1.8e10, 34 * MIB, PDEV * NYS),
        name="nys_parts",
    )(centres, nys_t)


def correct_kernel(pred_ref, targ_ref, modes_ref, eig_ref, resid_ref, tiles_ref):
    total = pred_ref[0]
    for i in range(1, NCOL):
        total = total + pred_ref[i]
    resid = total - targ_ref[...]
    for i in range(NROW):
        resid_ref[i] = resid
    coeff = jnp.dot(
        resid, modes_ref[...], precision=lax.Precision.HIGHEST, preferred_element_type=F32
    )
    per = NCOL // NROW
    for r in range(NROW):
        share = jnp.dot(
            coeff, eig_ref[r], precision=lax.Precision.HIGHEST, preferred_element_type=F32
        )
        for k in range(per):
            tiles_ref[r * per + k] = share[:, k * 128 : (k + 1) * 128]


def correct(pred, targ, modes, eig):
    return pl.pallas_call(
        correct_kernel,
        out_shape=[
            jax.ShapeDtypeStruct((NROW, 8, BATCH), F32),
            jax.ShapeDtypeStruct((NCOL, 8, 128), F32),
        ],
        compiler_params=params(grid=0),
        cost_estimate=cost(1e8, 2 * MIB),
        name="correct",
    )(pred, targ, modes, eig)


def direct_kernel(hi_ref, lo_ref, resid_ref, out_ref, outr_ref):
    rhi, rlo = split2(resid_ref[...])
    out_ref[...] = dot_nt(hi_ref[...], rhi) + dot_nt(hi_ref[...], rlo) + dot_nt(lo_ref[...], rhi)
    outr_ref[...] = resid_ref[...].T


def direct_part(hi, lo, resid_t):
    return pl.pallas_call(
        direct_kernel,
        out_shape=[
            jax.ShapeDtypeStruct((PDEV, OUTS), F32),
            jax.ShapeDtypeStruct((BATCH, OUTS), F32),
        ],
        compiler_params=params(grid=0),
        cost_estimate=cost(1e9, 5 * MIB),
        name="direct_part",
    )(hi, lo, resid_t)


def step_kernel(core_ref, own_ref, other_ref, hi_ref, lo_ref, direct_ref, out_ref, corr, parts):
    @pl.when(pl.program_id(0) == 0)
    def _():
        place_tiles(core_ref, own_ref, other_ref, corr)
        hi, lo = split2(corr[...])
        parts[:OUTS] = hi
        parts[OUTS:] = lo

    both = dot_nt(hi_ref[...], parts[...])
    back = both[:, :OUTS] + both[:, OUTS:] + dot_nt(lo_ref[...], parts[:OUTS])
    out_ref[...] = RATE * (direct_ref[...] - back)


def step_of(core, own, other, hi, lo, direct):
    rows = 256
    whole = pl.BlockSpec((NCHIPS, 8, 128), lambda i: (0, 0, 0))
    return pl.pallas_call(
        step_kernel,
        grid=(PDEV // rows,),
        in_specs=[
            pl.BlockSpec(memory_space=pltpu.SMEM),
            whole,
            whole,
            pl.BlockSpec((rows, NYS), lambda i: (i, 0)),
            pl.BlockSpec((rows, NYS), lambda i: (i, 0)),
            pl.BlockSpec((rows, OUTS), lambda i: (i, 0)),
        ],
        out_specs=pl.BlockSpec((rows, OUTS), lambda i: (i, 0)),
        out_shape=jax.ShapeDtypeStruct((PDEV, OUTS), F32),
        scratch_shapes=[pltpu.VMEM((OUTS, NYS), F32), pltpu.VMEM((2 * OUTS, NYS), BF16)],
        compiler_params=params(),
        cost_estimate=cost(1.2e10, 36 * MIB),
        name="step_of",
    )(core, own, other, hi, lo, direct)


def swap(parts, axes):
    return lax.all_to_all(parts, axes, 0, 0, tiled=True)


def to_all(tiles):
    own = swap(tiles, CHIPS)
    other = lax.ppermute(own, "core", [(0, 1), (1, 0)])
    return own, other


def local(centres, weights, targets, batch_index, nystrom_index, eigvecs, mode_scale):
    offset = lax.axis_index(ALL) * PDEV
    core = jnp.full((1,), lax.axis_index("core"), jnp.int32)
    row = lax.axis_index(ROW)

    feats = select((batch_index - offset)[None, :], centres)
    feats = swap(feats.reshape(NROW, 8, BATCH), ROW)
    feats = swap(add_spread(feats, NCOL), COL)
    feats = swap(add_spread(feats, NROW), ROW)
    batch_t = feats.reshape(FEATS, BATCH)

    eig = swap(jnp.broadcast_to(eigvecs.T[None], (NROW, MODES, NYS // NROW)), ROW)

    nys = select((nystrom_index - offset)[None, :], centres)
    nys = swap(nys.reshape(NROW, 8, NYS), ROW)
    nys = swap(add_tiles(nys), COL)
    nys_t = assemble(core, *to_all(add_spread(nys, NCHIPS)))

    pred, khi, klo = batch_products(centres, batch_t, weights)
    pred = swap(pred.reshape(NROW, 8, BATCH), ROW)
    pred = swap(add_spread(pred, NCOL), COL)

    modes = mode_products(batch_t, nys_t, eig, mode_scale[None, :])
    targ = lax.dynamic_slice_in_dim(targets, row * 8, 8, 1).T
    resid, tiles = correct(pred, targ, modes, eig)
    tiles = swap(tiles, COL)
    own, other = to_all(add_spread(tiles, NCHIPS))

    nhi, nlo = nys_parts(centres, nys_t)
    resid_t = swap(resid, ROW).reshape(OUTS, BATCH)
    direct, residual = direct_part(khi, klo, resid_t)
    step = step_of(core, own, other, nhi, nlo, direct)
    return residual, step


def solution(mesh):
    fine = Mesh(mesh.devices.reshape(NX, NCORE, 8, 4), ALL)
    in_specs = (
        P(ALL, None),
        P(ALL, None),
        P(),
        P(),
        P(),
        P(ROW, COL),
        P(COL),
    )
    out_specs = (P(), P(ALL, None))
    return jax.shard_map(local, mesh=fine, in_specs=in_specs, out_specs=out_specs, check_vma=False)
```

time: 798 us -> 262 us (0.33)
  waiting for transfers between devices: 632 us -> 43.2 us
  matrix products: 94.6 us -> 0 us
  Pallas kernels: 0 us -> 71.6 us
  blocking collectives: 22.5 us -> 75 us
  starting transfers between devices: 0.34 us -> 52.3 us
  between operations: 13.9 us -> 0.83 us
  other arithmetic: 11.8 us -> 1.45 us
    psum x3 -> x0, waiting for transfers between devices: 632 us -> none  [the longest x1 260 us: local(): prediction = lax.psum(partial_pred, ('row', 'col'))]
    dot_general x9 -> x0, matrix products: 94.6 us -> none  [the longest x4 51.3 us: product(): jnp.dot(left, right, precision=lax.Precision.HIGHEST, preferred_element_t...]
    all_to_all x0 -> x4, blocking collectives: none -> 75 us  [swap(): return lax.all_to_all(parts, axes, 0, 0, tiled=True)]
    pallas_call x0 -> x15, Pallas kernels: none -> 71.6 us  [the longest x1 22.6 us: nys_parts(): pl.pallas_call(nys_kernel, grid=(PDEV // rows, NYS // block), in_specs=[p...]
    all_to_all x0 -> x8, starting transfers between devices: none -> 51.8 us  [swap(): return lax.all_to_all(parts, axes, 0, 0, tiled=True)]
    all_to_all x0 -> x8, waiting for transfers between devices: none -> 43.2 us  [swap(): return lax.all_to_all(parts, axes, 0, 0, tiled=True)]
    psum x1 -> x0, blocking collectives: 22.5 us -> none  [local(): coeff = mode_scale[:, None] * lax.psum(mode_terms, 'row')]
    gather x2 -> x0, local copies, waits for them, and re-layouts: 15.2 us -> none  [select_rows(): fetched = jnp.take(centres, jnp.clip(local_rows, 0, rows_dev - 1), axis=0)]
  transfers between devices with their start and end apart: 4 -> 10, of which waited for: 3 -> 7; matrix products, arithmetic and copies ran while one was open for 6% -> 1% of each run, Pallas kernels for 0% -> 20%
where the time goes in v1:
time: 262 us; the launch traced here: 260 us
  blocking collectives  75 us (29%)
  Pallas kernels  71.6 us (27%)
  starting transfers between devices  52.3 us (20%)
  waiting for transfers between devices  43.2 us (16%)
  local copies, waits for them, and re-layouts  16 us (6%)
    all_to_all x4, blocking collectives, swap(): return lax.all_to_all(parts, axes, 0, 0, tiled=True)  75 us
    all_to_all x8, starting transfers between devices, swap(): return lax.all_to_all(parts, axes, 0, 0, tiled=True)  51.8 us
    all_to_all x8, waiting for transfers between devices, swap(): return lax.all_to_all(parts, axes, 0, 0, tiled=True)  43.2 us
    pallas_call x1, Pallas kernels, nys_parts(): pl.pallas_call(nys_kernel, grid=(PDEV // rows, NYS // block), in_specs=[p...  22.6 us
    pallas_call x1, Pallas kernels, step_of(): pl.pallas_call(step_kernel, grid=(PDEV // rows,), in_specs=[pl.BlockSpec(...  16.6 us
    unnamed x28, local copies, waits for them, and re-layouts  14.3 us
    pallas_call x1, Pallas kernels, mode_products(): pl.pallas_call(modes_kernel, grid=(NROW,), in_specs=[pl.BlockSpec((FEATS,...  13.3 us
    pallas_call x2, Pallas kernels, select(): pl.pallas_call(select_kernel, grid=(n // block,), in_specs=[pl.BlockSpec(...  6.66 us
  transfers between devices with their start and end apart: 10, of which 7 were waited for; matrix products, arithmetic and copies ran while one was open for 1% of the time, Pallas kernels for 20%

profile of v1, /device:TPU:1, one launch (start us, length us, event | category | flops | bytes accessed | tf_op | source)
XLA Modules:
  0.0 260.5 jit_solution(3583998236107483811)
XLA Ops:
  0.7 1.4 copy.10.cent_ref
  3.6 10.9 %all_to_all.60.in_ref = f32[8,8,512]{2,1,0:T(8,128)S(1)} all-to-all(f32[8,8,512]{2,1,0:T(8,128)S(1)} %bitcast.15), channel_id=1, replica_groups=mesh['x'=4,'core'=2,'z'=8,'y'=4] {'x','core'}, dimensions={0} | all-to-all | bytes 262144 | tf_op jit(solution)/shard_map/all_to_all | solution.py:356
  15.3 11.2 %all-to-all-start.1 = ((f32[32,8,512]{2,1,0:T(8,128)}), f32[32,8,512]{2,1,0:T(8,128)S(1)}, u32[]{:S(2)}, u32[]{:S(2)}) async-start(f32[32,8,512]{2,1,0:T(8,128)} %add_spread.5), calls=%async_computation.1 | async-start | bytes 1048576 | tf_op jit(solution)/shard_map/all_to_all | solution.py:356
  27.2 5.9 %select.3 = f32[64,4096]{1,0:T(8,128)} custom-call(s32[1,4096]{1,0:T(1,128)S(1)} %bitcast.16, f32[2048,64]{1,0:T(8,128)S(1)} %copy.10.cent_ref), custom_call_target="tpu_custom_call" | custom-call | flops 3221225472 | bytes 1572864 | tf_op jit(solution)/shard_map/select/pallas_call | solution.py:85
  33.2 8.8 %all-to-all-done.1.in_ref = f32[32,8,512]{2,1,0:T(8,128)S(1)} async-done(((f32[32,8,512]{2,1,0:T(8,128)}), f32[32,8,512]{2,1,0:T(8,128)S(1)}, u32[]{:S(2)}, u32[]{:S(2)}) %all-to-all-start.1) | async-done | bytes 524320 | tf_op jit(solution)/shard_map/all_to_all | solution.py:356
  42.0 6.8 %all-to-all-start.5 = ((f32[8,8,4096]{2,1,0:T(8,128)}), f32[8,8,4096]{2,1,0:T(8,128)S(1)}, u32[]{:S(2)}, u32[]{:S(2)}) async-start(f32[8,8,4096]{2,1,0:T(8,128)} %bitcast.7), calls=%async_computation.5 | async-start | bytes 2097152 | tf_op jit(solution)/shard_map/all_to_all | solution.py:356
  49.5 14.4 %all-to-all-done.5.in_ref = f32[8,8,4096]{2,1,0:T(8,128)S(1)} async-done(((f32[8,8,4096]{2,1,0:T(8,128)}), f32[8,8,4096]{2,1,0:T(8,128)S(1)}, u32[]{:S(2)}, u32[]{:S(2)}) %all-to-all-start.5) | async-done | bytes 1048608 | tf_op jit(solution)/shard_map/all_to_all | solution.py:356
  63.9 4.1 %all-to-all-start.2 = ((f32[8,8,512]{2,1,0:T(8,128)}), f32[8,8,512]{2,1,0:T(8,128)S(1)}, u32[]{:S(2)}, u32[]{:S(2)}) async-start(f32[8,8,512]{2,1,0:T(8,128)} %add_spread.6), calls=%async_computation.2 | async-start | bytes 262144 | tf_op jit(solution)/shard_map/all_to_all | solution.py:356
  68.0 1.3 copy.11.wts_ref
  70.0 3.3 %all-to-all-done.2 = f32[8,8,512]{2,1,0:T(8,128)S(1)} async-done(((f32[8,8,512]{2,1,0:T(8,128)}), f32[8,8,512]{2,1,0:T(8,128)S(1)}, u32[]{:S(2)}, u32[]{:S(2)}) %all-to-all-start.2) | async-done | bytes 131104 | tf_op jit(solution)/shard_map/all_to_all | solution.py:356
  73.3 4.3 %all-to-all-start.6 = ((f32[32,8,128]{2,1,0:T(8,128)}), f32[32,8,128]{2,1,0:T(8,128)S(1)}, u32[]{:S(2)}, u32[]{:S(2)}) async-start(f32[32,8,128]{2,1,0:T(8,128)} %add_tiles.1), calls=%async_computation.6 | async-start | bytes 262144 | tf_op jit(solution)/shard_map/all_to_all | solution.py:356
  78.9 1.2 copy-done.7
  80.1 4.5 %batch_products.1 = (f32[64,512]{1,0:T(8,128)}, bf16[2048,512]{1,0:T(8,128)(2,1)S(1)}, bf16[2048,512]{1,0:T(8,128)(2,1)}) custom-call(f32[2048,64]{1,0:T(8,128)S(1)} %copy-done.5, f32[64,512]{1,0:T(8,128)S(1)} %bitcast.13, f32[2048,64]{1,0:T(8,128)S(1)} %copy-done.7), custom_call_target="tpu_custom_call" | custom-call | flops 6000000000 | bytes 6291456 | tf_op jit(solution)/shard_map/batch_products/pallas_call | solution.py:181
  84.6 2.4 all-to-all-done.6.in_ref
  87.0 5.6 %all-to-all-start.3 = ((f32[8,8,512]{2,1,0:T(8,128)}), f32[8,8,512]{2,1,0:T(8,128)S(1)}, u32[]{:S(2)}, u32[]{:S(2)}) async-start(f32[8,8,512]{2,1,0:T(8,128)} %bitcast.3), calls=%async_computation.3 | async-start | bytes 262144 | tf_op jit(solution)/shard_map/all_to_all | solution.py:356
  92.7 5.2 %all-to-all-done.3.in_ref = f32[8,8,512]{2,1,0:T(8,128)S(1)} async-done(((f32[8,8,512]{2,1,0:T(8,128)}), f32[8,8,512]{2,1,0:T(8,128)S(1)}, u32[]{:S(2)}, u32[]{:S(2)}) %all-to-all-start.3) | async-done | bytes 131104 | tf_op jit(solution)/shard_map/all_to_all | solution.py:356
  97.9 24.9 %all_to_all.61.own_ref = f32[128,8,128]{2,1,0:T(8,128)S(1)} all-to-all(f32[128,8,128]{2,1,0:T(8,128)S(1)} %add_spread.8), channel_id=1, replica_groups=mesh['x'=4,'core'=2,'z'=8,'y'=4] {'x','z','y'}, dimensions={0} | all-to-all | bytes 1048576 | tf_op jit(solution)/shard_map/all_to_all | solution.py:356
  122.8 1.7 broadcast_in_dim.21
  124.5 6.8 %all-to-all-start.8 = ((f32[8,32,512]{2,1,0:T(8,128)}), f32[8,32,512]{2,1,0:T(8,128)S(1)}, u32[]{:S(2)}, u32[]{:S(2)}) async-start(f32[8,32,512]{2,1,0:T(8,128)} %broadcast_in_dim.21), calls=%async_computation.8 | async-start | bytes 1048576 | tf_op jit(solution)/shard_map/all_to_all | solution.py:356
  132.4 8.4 %all-to-all-done.8.eig_ref = f32[8,32,512]{2,1,0:T(8,128)S(1)} async-done(((f32[8,32,512]{2,1,0:T(8,128)}), f32[8,32,512]{2,1,0:T(8,128)S(1)}, u32[]{:S(2)}, u32[]{:S(2)}) %all-to-all-start.8) | async-done | bytes 524320 | tf_op jit(solution)/shard_map/all_to_all | solution.py:356
  140.8 4.6 %all-to-all-start.4 = ((f32[32,8,512]{2,1,0:T(8,128)}), f32[32,8,512]{2,1,0:T(8,128)}, u32[]{:S(2)}, u32[]{:S(2)}) async-start(f32[32,8,512]{2,1,0:T(8,128)} %add_spread.7), calls=%async_computation.4 | async-start | bytes 1048576 | tf_op jit(solution)/shard_map/all_to_all | solution.py:356
  146.6 13.3 %mode_products.1.modes_ref = f32[512,32]{1,0:T(8,128)S(1)} custom-call(f32[64,512]{1,0:T(8,128)S(1)} %bitcast.14, f32[64,4096]{1,0:T(8,128)S(1)} %assemble.1.nys_ref, f32[8,32,512]{2,1,0:T(8,128)S(1)} %all-to-all-done.8.eig_ref, f32[1,32]{1,0:T(1,128)S(1)} %bitcast.18), custom_call_target="tpu_custom_call" | custom-call | flops 10000000000 | bytes 3145728 | tf_op jit(solution)/shard_map/mode_products/pallas_call | solution.py:227
  161.5 1.8 correct.1
  163.3 17.7 %all_to_all.62.in_ref = f32[32,8,128]{2,1,0:T(8,128)S(1)} all-to-all(f32[32,8,128]{2,1,0:T(8,128)S(1)} %get-tuple-element.16), channel_id=1, replica_groups=mesh['x'=4,'core'=2,'z'=8,'y'=4] {'z','y'}, dimensions={0} | all-to-all | bytes 262144 | tf_op jit(solution)/shard_map/all_to_all | solution.py:356
  181.1 21.5 %all_to_all.63.own_ref = f32[128,8,128]{2,1,0:T(8,128)} all-to-all(f32[128,8,128]{2,1,0:T(8,128)S(1)} %add_spread.9), channel_id=1, replica_groups=mesh['x'=4,'core'=2,'z'=8,'y'=4] {'x','z','y'}, dimensions={0} | all-to-all | bytes 1048576 | tf_op jit(solution)/shard_map/all_to_all | solution.py:356
  202.6 8.4 %all-to-all-start.9 = ((f32[8,8,512]{2,1,0:T(8,128)}), f32[8,8,512]{2,1,0:T(8,128)S(1)}, u32[]{:S(2)}, u32[]{:S(2)}) async-start(f32[8,8,512]{2,1,0:T(8,128)} %get-tuple-element.14), calls=%async_computation.9 | async-start | bytes 262144 | tf_op jit(solution)/shard_map/all_to_all | solution.py:356
  211.3 1.2 copy-done.3
  213.8 22.6 %nys_parts.1 = (bf16[2048,4096]{1,0:T(8,128)(2,1)}, bf16[2048,4096]{1,0:T(8,128)(2,1)}) custom-call(f32[2048,64]{1,0:T(8,128)S(1)} %copy-done.6, f32[64,4096]{1,0:T(8,128)S(1)} %copy-done.3), custom_call_target="tpu_custom_call" | custom-call | flops 17999998976 | bytes 35651584 | tf_op jit(solution)/shard_map/nys_parts/pallas_call | solution.py:253
  236.4 1.6 copy-done.1
  238.0 1.8 direct_part.1
  241.5 1.2 copy-done.9
  242.8 16.6 %step_of.1 = f32[2048,64]{1,0:T(8,128)S(1)} custom-call(s32[1]{0:T(128)} %bitcast.5.core_ref, f32[128,8,128]{2,1,0:T(8,128)} %all_to_all.63.own_ref, f32[128,8,128]{2,1,0:T(8,128)} %collective-permute-done.1.other_ref, bf16[2048,4096]{1,0:T(8,128)(2,1)} %get-tuple-element.17.hi_ref, bf16[2048,4096]{1,0:T(8,128)(2,1)} %get-tuple-element.18.lo_ref, ...), custom_call_target="tpu_custom_call" | custom-call | flops 12000000000 | bytes 37748736 | tf_op jit(solution)/shard_map/step_of/pallas_call | solution.py:335
  (39 shorter events, 14.1 us)
Async XLA Ops:
  0.6 144.8 %copy-start = (f32[512,64]{0,1:T(8,128)S(1)}, f32[512,64]{0,1:T(8,128)}, u32[]{:S(2)}) copy-start(f32[512,64]{0,1:T(8,128)} %param.9) | copy-start | bytes 393220
  0.6 67.4 %copy-start.11 = (f32[2048,64]{0,1:T(8,128)S(1)}, f32[2048,64]{0,1:T(8,128)}, u32[]{:S(2)}) copy-start(f32[2048,64]{0,1:T(8,128)} %param.8) | copy-start | bytes 1572868
  2.1 39.9 %copy-start.4 = (f32[2048,64]{1,0:T(8,128)}, f32[2048,64]{1,0:T(8,128)S(1)}, u32[]{:S(2)}) copy-start(f32[2048,64]{1,0:T(8,128)S(1)} %copy.10.cent_ref) | copy-start | bytes 1572868
  15.3 26.6 %all-to-all-start.1 = ((f32[32,8,512]{2,1,0:T(8,128)}), f32[32,8,512]{2,1,0:T(8,128)S(1)}, u32[]{:S(2)}, u32[]{:S(2)}) async-start(f32[32,8,512]{2,1,0:T(8,128)} %add_spread.5), calls=%async_computation.1 | async-start | bytes 1048576 | tf_op jit(solution)/shard_map/all_to_all | solution.py:356
  42.0 21.9 %all-to-all-start.5 = ((f32[8,8,4096]{2,1,0:T(8,128)}), f32[8,8,4096]{2,1,0:T(8,128)S(1)}, u32[]{:S(2)}, u32[]{:S(2)}) async-start(f32[8,8,4096]{2,1,0:T(8,128)} %bitcast.7), calls=%async_computation.5 | async-start | bytes 2097152 | tf_op jit(solution)/shard_map/all_to_all | solution.py:356
  48.7 97.9 %copy-start.10 = (f32[32]{0:T(128)S(1)}, f32[32]{0:T(128)}, u32[]{:S(2)}) copy-start(f32[32]{0:T(128)} %param.13) | copy-start | bytes 388
  63.9 9.4 %all-to-all-start.2 = ((f32[8,8,512]{2,1,0:T(8,128)}), f32[8,8,512]{2,1,0:T(8,128)S(1)}, u32[]{:S(2)}, u32[]{:S(2)}) async-start(f32[8,8,512]{2,1,0:T(8,128)} %add_spread.6), calls=%async_computation.2 | async-start | bytes 262144 | tf_op jit(solution)/shard_map/all_to_all | solution.py:356
  73.3 13.7 %all-to-all-start.6 = ((f32[32,8,128]{2,1,0:T(8,128)}), f32[32,8,128]{2,1,0:T(8,128)S(1)}, u32[]{:S(2)}, u32[]{:S(2)}) async-start(f32[32,8,128]{2,1,0:T(8,128)} %add_tiles.1), calls=%async_computation.6 | async-start | bytes 262144 | tf_op jit(solution)/shard_map/all_to_all | solution.py:356
  77.6 1.2 copy-start.5
  78.9 1.2 copy-start.7
  87.0 10.9 %all-to-all-start.3 = ((f32[8,8,512]{2,1,0:T(8,128)}), f32[8,8,512]{2,1,0:T(8,128)S(1)}, u32[]{:S(2)}, u32[]{:S(2)}) async-start(f32[8,8,512]{2,1,0:T(8,128)} %bitcast.3), calls=%async_computation.3 | async-start | bytes 262144 | tf_op jit(solution)/shard_map/all_to_all | solution.py:356
  124.5 16.3 %all-to-all-start.8 = ((f32[8,32,512]{2,1,0:T(8,128)}), f32[8,32,512]{2,1,0:T(8,128)S(1)}, u32[]{:S(2)}, u32[]{:S(2)}) async-start(f32[8,32,512]{2,1,0:T(8,128)} %broadcast_in_dim.21), calls=%async_computation.8 | async-start | bytes 1048576 | tf_op jit(solution)/shard_map/all_to_all | solution.py:356
  131.3 14.2 %collective-permute-start = (f32[128,8,128]{2,1,0:T(8,128)S(1)}, f32[128,8,128]{2,1,0:T(8,128)}, u32[]{:S(2)}, u32[]{:S(2)}) collective-permute-start(f32[128,8,128]{2,1,0:T(8,128)S(1)} %all_to_all.61.own_ref), channel_id=1, source_target_pairs={{0,32},{32,0},{1,33},{33,1},{2,34},{34,2},{3,35},{35,3},{4,36},{36... | collective-permute-start | bytes 1572872 | tf_op jit(solution)/shard_map/ppermute | solution.py:361
  140.8 20.7 %all-to-all-start.4 = ((f32[32,8,512]{2,1,0:T(8,128)}), f32[32,8,512]{2,1,0:T(8,128)}, u32[]{:S(2)}, u32[]{:S(2)}) async-start(f32[32,8,512]{2,1,0:T(8,128)} %add_spread.7), calls=%async_computation.4 | async-start | bytes 1048576 | tf_op jit(solution)/shard_map/all_to_all | solution.py:356
  159.9 1.0 copy-start.2
  202.6 33.8 %all-to-all-start.9 = ((f32[8,8,512]{2,1,0:T(8,128)}), f32[8,8,512]{2,1,0:T(8,128)S(1)}, u32[]{:S(2)}, u32[]{:S(2)}) async-start(f32[8,8,512]{2,1,0:T(8,128)} %get-tuple-element.14), calls=%async_computation.9 | async-start | bytes 262144 | tf_op jit(solution)/shard_map/all_to_all | solution.py:356
  210.9 30.6 %collective-permute-start.1 = (f32[128,8,128]{2,1,0:T(8,128)}, f32[128,8,128]{2,1,0:T(8,128)}, u32[]{:S(2)}, u32[]{:S(2)}) collective-permute-start(f32[128,8,128]{2,1,0:T(8,128)} %all_to_all.63.own_ref), channel_id=1, source_target_pairs={{0,32},{32,0},{1,33},{33,1},{2,34},{34,2},{3,35},{35,3},{4,36},{36... | collective-permute-start | bytes 1572872 | tf_op jit(solution)/shard_map/ppermute | solution.py:361
  211.3 1.2 copy-start.3
  212.5 1.2 copy-start.6
  236.4 1.6 copy-start.1
  239.8 1.0 copy-start.8
  241.5 1.2 copy-start.9
